TPU v7x, 512 devices: a whole 4x8x8 slice. The times are simulated.
512 devices in a mesh: node: 64 (over x, z, core), local: 8 (over y).
Axes of the slice: x: 4, y: 8, z: 8, core: 2. Of those that a mesh axis runs over, the one named last changes fastest.
Arguments:
- master_weight: bfloat16 [64, 128, 2048], P(None, 'node', 'local'), may hold values from -6 to 6
- first_moment: float32 [64, 128, 2048], P(None, 'node', 'local'), may hold values from -6 to 6
- second_moment: float32 [64, 128, 2048], P(None, 'node', 'local'), may hold values from 0.25 to 4
- features: bfloat16 [128, 8, 128, 128], P('node', 'local'), may hold values from -6 to 6
- grad_out: bfloat16 [128, 8, 128, 2048], P('node', 'local'), may hold values from -0.1875 to 0.1875
- old_place: int32 [80], replicated, may hold values from 0 to 127, as said below
- new_place: int32 [80], replicated, may hold values from 0 to 127, as said below
- old_owner: int32 [16], replicated, may hold values from 0 to 63
- new_owner: int32 [16], replicated, may hold values from 0 to 63
Outputs:
- slot_weight: bfloat16 [128, 128, 2048], P('node', None, 'local')
- slot_first: float32 [128, 128, 2048], P('node', None, 'local')
- slot_second: float32 [128, 128, 2048], P('node', None, 'local')
Inputs may be any that keep to these rules, and one draw needn't show every extreme that they name: `old_place`: 80 distinct positions; position p belongs to node p // 2; in every draw some node has all 2 of its positions taken. `new_place`: 80 distinct positions; position p belongs to node p // 2; in every draw some node has all 2 of its positions taken.
All inputs are finite; a program needn't handle non-finite values.
Results may differ from a plain program's by a relative error of at most 0.0044.
Values may be sent and summed in bfloat16 or wider, within the bound.
A program may use at most 64 MiB of HBM per device.

v0:
```python
import jax
import jax.numpy as jnp
from jax import lax
from jax.sharding import PartitionSpec as P

BETA_FIRST = 0.9
BETA_SECOND = 0.95
LEARNING_RATE = 0.1
DECAY_RATE = 0.1
EPSILON = 1e-08
CORRECT_FIRST = 1.0 - 0.9**10
CORRECT_SECOND = 1.0 - 0.95**10


def one_hot(values, length):
    return (values[:, None] == jnp.arange(length, dtype=jnp.int32)[None, :]).astype(jnp.float32)


def local(
    master_weight,
    first_moment,
    second_moment,
    features,
    grad_out,
    old_place,
    new_place,
    old_owner,
    new_owner,
):
    node_count = lax.axis_size("node")
    capacity = features.shape[0]
    experts = master_weight.shape[0]
    block_rows = master_weight.shape[1]
    columns = master_weight.shape[2]
    hidden_width = grad_out.shape[3]
    positions = node_count * capacity
    primaries = jnp.arange(experts, dtype=jnp.int32)
    old_expert = jnp.concatenate([primaries, old_owner])
    new_expert = jnp.concatenate([primaries, new_owner])
    slot_grad = jnp.einsum("cltr,cltf->crf", features, grad_out, preferred_element_type=jnp.float32)
    collect = jnp.dot(
        one_hot(old_expert, experts).T,
        one_hot(old_place, positions),
        precision=lax.Precision.HIGHEST,
    )
    collect = collect.reshape(experts, node_count, capacity)
    blocks = lax.all_to_all(
        slot_grad.reshape(capacity, node_count, block_rows, hidden_width).astype(jnp.bfloat16),
        "node",
        split_axis=1,
        concat_axis=1,
        tiled=True,
    ).astype(jnp.float32)
    summed = jnp.einsum(
        "ekc,ckx->ex",
        collect,
        blocks.reshape(capacity, node_count, block_rows * hidden_width),
        precision=lax.Precision.HIGHEST,
    )
    gradient = lax.psum_scatter(
        summed.reshape(experts, block_rows, hidden_width).astype(jnp.bfloat16),
        "local",
        scatter_dimension=2,
        tiled=True,
    ).astype(jnp.float32)
    first_new = BETA_FIRST * first_moment + (1.0 - BETA_FIRST) * gradient
    second_new = BETA_SECOND * second_moment + (1.0 - BETA_SECOND) * gradient * gradient
    weight_old = master_weight.astype(jnp.float32)
    update = (
        first_new / CORRECT_FIRST / (jnp.sqrt(second_new / CORRECT_SECOND) + EPSILON)
        + DECAY_RATE * weight_old
    )
    weight_new = (weight_old - LEARNING_RATE * update).astype(jnp.bfloat16)
    choose = jnp.dot(
        one_hot(new_place, positions).T,
        one_hot(new_expert, experts),
        precision=lax.Precision.HIGHEST,
    )
    choose = choose.reshape(node_count, capacity, experts)
    flat_size = block_rows * columns
    send_weight = jnp.einsum(
        "nce,ex->cnx",
        choose.astype(jnp.bfloat16),
        weight_new.reshape(experts, flat_size),
        preferred_element_type=jnp.float32,
    ).astype(jnp.bfloat16)
    send_first = jnp.einsum(
        "nce,ex->cnx",
        choose,
        first_new.reshape(experts, flat_size),
        precision=lax.Precision.HIGHEST,
    )
    send_second = jnp.einsum(
        "nce,ex->cnx",
        choose,
        second_new.reshape(experts, flat_size),
        precision=lax.Precision.HIGHEST,
    )
    got_weight = lax.all_to_all(
        send_weight.reshape(capacity, node_count, block_rows, columns),
        "node",
        split_axis=1,
        concat_axis=1,
        tiled=True,
    )
    got_first, got_second = (
        lax.all_to_all(
            send_first.reshape(capacity, node_count, block_rows, columns),
            "node",
            split_axis=1,
            concat_axis=1,
            tiled=True,
        ),
        lax.all_to_all(
            send_second.reshape(capacity, node_count, block_rows, columns),
            "node",
            split_axis=1,
            concat_axis=1,
            tiled=True,
        ),
    )
    all_rows = node_count * block_rows
    return (
        got_weight.reshape(capacity, all_rows, columns),
        got_first.reshape(capacity, all_rows, columns),
        got_second.reshape(capacity, all_rows, columns),
    )


def solution(mesh):
    return jax.shard_map(
        local,
        mesh=mesh,
        in_specs=(
            P(None, "node", "local"),
            P(None, "node", "local"),
            P(None, "node", "local"),
            P("node", "local", None, None),
            P("node", "local", None, None),
            P(),
            P(),
            P(),
            P(),
        ),
        out_specs=(P("node", None, "local"), P("node", None, "local"), P("node", None, "local")),
        check_vma=False,
    )
```

profile of v0, /device:TPU:1, one launch (start us, length us, event | category | flops | bytes accessed | tf_op | source)
XLA Modules:
  0.0 161.8 jit_solution(17696610270887174766)
XLA Ops:
  7.2 1.2 copy-done
  8.4 1.3 convolution_convert_fusion
  9.7 0.7 convert_element_type.37
  10.4 2.2 %copy.59 = bf16[2,64,2,2048]{3,2,0,1:T(2,128)(2,1)} copy(bf16[2,64,2,2048]{3,2,1,0:T(2,128)(2,1)S(1)} %convert_element_type.37) | data formatting | bytes 2097152 | tf_op jit(solution)/shard_map/convert_element_type | solution.py:48
  12.7 15.0 %all-to-all-start = ((bf16[2,64,2,2048]{3,2,0,1:T(2,128)(2,1)}), bf16[2,64,2,2048]{3,2,0,1:T(2,128)(2,1)S(1)}, u32[]{:S(2)}, u32[]{:S(2)}) async-start(bf16[2,64,2,2048]{3,2,0,1:T(2,128)(2,1)} %copy.59), calls=%async_computation | async-start | bytes 2097152 | tf_op jit(solution)/shard_map/all_to_all | solution.py:47
  27.8 0.3 fusion.14
  28.2 28.0 %all-to-all-done = bf16[2,64,2,2048]{3,2,0,1:T(2,128)(2,1)S(1)} async-done(((bf16[2,64,2,2048]{3,2,0,1:T(2,128)(2,1)}), bf16[2,64,2,2048]{3,2,0,1:T(2,128)(2,1)S(1)}, u32[]{:S(2)}, u32[]{:S(2)}) %all-to-all-start) | async-done | bytes 1048608 | tf_op jit(solution)/shard_map/all_to_all | solution.py:47
  56.2 0.8 reshape.60
  57.0 0.6 copy.60
  57.6 1.4 fusion
  59.1 0.3 fusion.23
  59.5 31.2 %reduce-scatter.2.cloned.1.call-done = bf16[64,2,256]{2,0,1:T(8,128)(2,1)} async-done(((bf16[64,2,2048]{2,0,1:T(8,128)(2,1)}), bf16[64,2,256]{2,0,1:T(8,128)(2,1)}) %reduce-scatter.2.cloned.1.call-update) | async-done | bytes 65552 | tf_op jit(solution)/shard_map/reduce_scatter | solution.py:60
  90.7 1.0 fusion.7
  91.8 0.2 fusion.1
  92.0 0.7 copy.67
  92.8 16.0 %all-to-all-start.1 = ((bf16[2,64,2,256]{3,2,0,1:T(2,128)(2,1)}), bf16[2,64,2,256]{3,2,0,1:T(2,128)(2,1)S(1)}, u32[]{:S(2)}, u32[]{:S(2)}) async-start(bf16[2,64,2,256]{3,2,0,1:T(2,128)(2,1)} %copy.67), calls=%async_computation.2 | async-start | bytes 262144 | tf_op jit(solution)/shard_map/all_to_all | solution.py:99
  109.1 0.4 convolution_bitcast_fusion.2
  109.5 0.2 reshape.66
  109.6 0.7 copy.72
  110.4 8.7 %all-to-all-done.1 = bf16[2,64,2,256]{3,2,0,1:T(2,128)(2,1)S(1)} async-done(((bf16[2,64,2,256]{3,2,0,1:T(2,128)(2,1)}), bf16[2,64,2,256]{3,2,0,1:T(2,128)(2,1)S(1)}, u32[]{:S(2)}, u32[]{:S(2)}) %all-to-all-start.1) | async-done | bytes 131104 | tf_op jit(solution)/shard_map/all_to_all | solution.py:99
  119.1 4.9 %all-to-all-start.2 = ((f32[2,64,2,256]{3,2,0,1:T(2,128)}), f32[2,64,2,256]{3,2,0,1:T(2,128)S(1)}, u32[]{:S(2)}, u32[]{:S(2)}) async-start(f32[2,64,2,256]{3,2,0,1:T(2,128)} %copy.72), calls=%async_computation.3 | async-start | bytes 524288 | tf_op jit(solution)/shard_map/all_to_all | solution.py:107
  124.2 0.4 convolution_bitcast_fusion.1
  124.6 0.2 reshape.69
  124.8 0.7 copy.76
  125.5 10.5 %all-to-all-done.2 = f32[2,64,2,256]{3,2,0,1:T(2,128)S(1)} async-done(((f32[2,64,2,256]{3,2,0,1:T(2,128)}), f32[2,64,2,256]{3,2,0,1:T(2,128)S(1)}, u32[]{:S(2)}, u32[]{:S(2)}) %all-to-all-start.2) | async-done | bytes 262176 | tf_op jit(solution)/shard_map/all_to_all | solution.py:107
  136.0 6.0 %all-to-all-start.3 = ((f32[2,64,2,256]{3,2,0,1:T(2,128)}), f32[2,64,2,256]{3,2,0,1:T(2,128)S(1)}, u32[]{:S(2)}, u32[]{:S(2)}) async-start(f32[2,64,2,256]{3,2,0,1:T(2,128)} %copy.76), calls=%async_computation.4 | async-start | bytes 524288 | tf_op jit(solution)/shard_map/all_to_all | solution.py:114
  142.2 0.7 copy.78
  142.8 0.1 copy.73
  143.0 0.7 copy.79
  143.7 10.4 %all-to-all-done.3 = f32[2,64,2,256]{3,2,0,1:T(2,128)S(1)} async-done(((f32[2,64,2,256]{3,2,0,1:T(2,128)}), f32[2,64,2,256]{3,2,0,1:T(2,128)S(1)}, u32[]{:S(2)}, u32[]{:S(2)}) %all-to-all-start.3) | async-done | bytes 262176 | tf_op jit(solution)/shard_map/all_to_all | solution.py:114
  154.0 0.1 copy.77
  154.2 0.7 copy.80
  (30 shorter events, 1.1 us)
Async XLA Ops:
  7.2 1.2 copy-start
  12.7 15.0 %copy-start.4 = (s32[16]{0:T(128)S(1)}, s32[16]{0:T(128)}, u32[]{:S(2)}) copy-start(s32[16]{0:T(128)} %param.17) | copy-start | bytes 196
  12.7 15.0 %copy-start.5 = (s32[16]{0:T(128)S(1)}, s32[16]{0:T(128)}, u32[]{:S(2)}) copy-start(s32[16]{0:T(128)} %param.16) | copy-start | bytes 196
  12.7 15.1 %copy-start.6 = (s32[80]{0:T(128)S(1)}, s32[80]{0:T(128)}, u32[]{:S(2)}) copy-start(s32[80]{0:T(128)} %param.14) | copy-start | bytes 964
  12.7 43.5 %all-to-all-start = ((bf16[2,64,2,2048]{3,2,0,1:T(2,128)(2,1)}), bf16[2,64,2,2048]{3,2,0,1:T(2,128)(2,1)S(1)}, u32[]{:S(2)}, u32[]{:S(2)}) async-start(bf16[2,64,2,2048]{3,2,0,1:T(2,128)(2,1)} %copy.59), calls=%async_computation | async-start | bytes 2097152 | tf_op jit(solution)/shard_map/all_to_all | solution.py:47
  27.6 63.1 %reduce-scatter.2.cloned.1.call-start = ((), (), s32[]{:S(2)}) async-start(), calls=%async_computation.5 | async-start | bytes 589824 | tf_op jit(solution)/shard_map/reduce_scatter | solution.py:60
  57.6 1.5 copy-start.7
  57.6 33.1 %copy-start.1 = (f32[64,2,256]{2,1,0:T(2,128)S(1)}, f32[64,2,256]{2,1,0:T(2,128)}, u32[]{:S(2)}) copy-start(f32[64,2,256]{2,1,0:T(2,128)} %param.10) | copy-start | bytes 393220
  57.6 33.1 %copy-start.2 = (f32[64,2,256]{2,1,0:T(2,128)S(1)}, f32[64,2,256]{2,1,0:T(2,128)}, u32[]{:S(2)}) copy-start(f32[64,2,256]{2,1,0:T(2,128)} %param.11) | copy-start | bytes 393220
  57.6 33.1 %copy-start.3 = (bf16[64,2,256]{2,1,0:T(2,128)(2,1)S(1)}, bf16[64,2,256]{2,1,0:T(2,128)(2,1)}, u32[]{:S(2)}) copy-start(bf16[64,2,256]{2,1,0:T(2,128)(2,1)} %param.9) | copy-start | bytes 196612
  92.8 26.4 %all-to-all-start.1 = ((bf16[2,64,2,256]{3,2,0,1:T(2,128)(2,1)}), bf16[2,64,2,256]{3,2,0,1:T(2,128)(2,1)S(1)}, u32[]{:S(2)}, u32[]{:S(2)}) async-start(bf16[2,64,2,256]{3,2,0,1:T(2,128)(2,1)} %copy.67), calls=%async_computation.2 | async-start | bytes 262144 | tf_op jit(solution)/shard_map/all_to_all | solution.py:99
  119.1 16.9 %all-to-all-start.2 = ((f32[2,64,2,256]{3,2,0,1:T(2,128)}), f32[2,64,2,256]{3,2,0,1:T(2,128)S(1)}, u32[]{:S(2)}, u32[]{:S(2)}) async-start(f32[2,64,2,256]{3,2,0,1:T(2,128)} %copy.72), calls=%async_computation.3 | async-start | bytes 524288 | tf_op jit(solution)/shard_map/all_to_all | solution.py:107
  136.0 18.0 %all-to-all-start.3 = ((f32[2,64,2,256]{3,2,0,1:T(2,128)}), f32[2,64,2,256]{3,2,0,1:T(2,128)S(1)}, u32[]{:S(2)}, u32[]{:S(2)}) async-start(f32[2,64,2,256]{3,2,0,1:T(2,128)} %copy.76), calls=%async_computation.4 | async-start | bytes 524288 | tf_op jit(solution)/shard_map/all_to_all | solution.py:114
Sparse Core Ops, SparseCore 0:
  59.2 31.4 reduce-scatter.1
where the time goes:
time: 162 us
  waiting for transfers between devices  88.9 us (55%)
  starting transfers between devices  41.9 us (26%)
  between operations  14.3 us (9%)
  local copies, waits for them, and re-layouts  11.5 us (7%)
  matrix products  4.18 us (3%)
    reduce_scatter x1, waiting for transfers between devices, local(): lax.psum_scatter(summed.reshape(experts, block_rows, hidden_width).astype...  31.2 us
    all_to_all x1, waiting for transfers between devices, local(): lax.all_to_all(slot_grad.reshape(capacity, node_count, block_rows, hidden...  28 us
    all_to_all x1, starting transfers between devices, local(): lax.all_to_all(send_weight.reshape(capacity, node_count, block_rows, colu...  16 us
    all_to_all x1, starting transfers between devices, local(): lax.all_to_all(slot_grad.reshape(capacity, node_count, block_rows, hidden...  15 us
    all_to_all x1, waiting for transfers between devices, local(): lax.all_to_all(send_first.reshape(capacity, node_count, block_rows, colum...  10.5 us
    all_to_all x1, waiting for transfers between devices, local(): lax.all_to_all(send_second.reshape(capacity, node_count, block_rows, colu...  10.4 us
    all_to_all x1, waiting for transfers between devices, local(): lax.all_to_all(send_weight.reshape(capacity, node_count, block_rows, colu...  8.74 us
    all_to_all x1, starting transfers between devices, local(): lax.all_to_all(send_second.reshape(capacity, node_count, block_rows, colu...  6.03 us
  transfers between devices with their start and end apart: 5, of which 5 were waited for; matrix products, arithmetic and copies ran while one was open for 3% of the time, Pallas kernels for 0%

commit v1 on v0

v1 whole, which is shorter than its diff:
```python
import functools

import jax
import jax.numpy as jnp
from jax import lax
from jax.experimental import pallas as pl
from jax.experimental.pallas import tpu as pltpu
from jax.sharding import PartitionSpec as P

BETA_FIRST = 0.9
BETA_SECOND = 0.95
LEARNING_RATE = 0.1
DECAY_RATE = 0.1
EPSILON = 1e-08
CORRECT_FIRST = 1.0 - 0.9**10
CORRECT_SECOND = 1.0 - 0.95**10

MESH = pl.DeviceIdType.MESH
LANES = 128
F32 = jnp.float32
BF16 = jnp.bfloat16


def dot(a, b):
    return jnp.dot(a, b, preferred_element_type=F32)


def dot_nt(a, b):
    return lax.dot_general(a, b, (((1,), (1,)), ((), ())), preferred_element_type=F32)


def equal(a, b):
    return jnp.where(a == b, 1.0, 0.0)


def iota(shape, axis):
    return lax.broadcasted_iota(jnp.int32, shape, axis)


def exchange(
    nodes,
    ring,
    meta_ref,
    weight_ref,
    first_ref,
    second_ref,
    features_ref,
    grad_ref,
    out_weight,
    out_first,
    out_second,
    out_grad,
    turned,
    ring_send,
    ring_recv,
    state_send,
    state_recv,
    rows_send,
    rows_recv,
    slots_send,
    slots_recv,
    total,
    order,
    match,
    ring_out_sem,
    ring_in_sem,
    out_sem,
    in_sem,
):
    node = lax.axis_index("node")
    place = lax.axis_index("local")
    experts = weight_ref.shape[0] // 4
    rows = features_ref.shape[2]
    columns = 2 * LANES
    tall = 8 * nodes
    half = ring // 2

    barrier = pltpu.get_barrier_semaphore()

    def greet(k, carry):
        pl.semaphore_signal(
            barrier, inc=1, device_id=(lax.rem(node + k, nodes), place), device_id_type=MESH
        )
        return carry

    lax.fori_loop(1, nodes, greet, 0)
    right = lax.rem(place + 1, ring)
    left = lax.rem(place + ring - 1, ring)
    for neighbour in (right, left):
        pl.semaphore_signal(barrier, inc=1, device_id=(node, neighbour), device_id_type=MESH)

    for c in range(2):
        turned[c] = features_ref[c].astype(F32).T.astype(BF16)

    def partial(c, ahead):
        block = lax.rem(place + ahead + ring, ring)
        at = pl.multiple_of(block * columns, columns)
        return dot(turned[c], grad_ref[c, :, pl.ds(at, columns)])

    chains = {(0, 1): half, (1, -1): half, (0, -1): half - 1, (1, 1): half - 1}
    slot = {}
    for key, length in chains.items():
        for k in range(length):
            slot[key + (k,)] = len(slot)

    def hop(c, way, k):
        j = slot[(c, way, k)]
        return pltpu.make_async_remote_copy(
            src_ref=ring_send.at[j],
            dst_ref=ring_recv.at[j],
            send_sem=ring_out_sem.at[j],
            recv_sem=ring_in_sem.at[j],
            device_id=(node, right if way == 1 else left),
            device_id_type=MESH,
        )

    def advance(c, way, k):
        if k >= chains[(c, way)]:
            return
        value = partial(c, way * (chains[(c, way)] - k))
        if k:
            hop(c, way, k - 1).wait_recv()
            value = value + ring_recv[slot[(c, way, k - 1)]].astype(F32)
        ring_send[slot[(c, way, k)]] = value.astype(BF16)
        if k:
            hop(c, way, k).start()

    for c, way in chains:
        advance(c, way, 0)
    pl.semaphore_wait(barrier, nodes + 1)
    for c, way in chains:
        hop(c, way, 0).start()

    def scatter(send, recv, which, first, last):
        def one(k, carry):
            other = lax.rem(node + k, nodes)
            pltpu.make_async_remote_copy(
                src_ref=send.at[other],
                dst_ref=recv.at[node],
                send_sem=out_sem.at[which],
                recv_sem=in_sem.at[which],
                device_id=(other, place),
                device_id_type=MESH,
            ).start()
            return carry

        lax.fori_loop(first, last, one, 0)

    def all_but_one(send, recv, which):
        return pltpu.make_async_remote_copy(
            src_ref=send.at[pl.ds(0, nodes - 1)],
            dst_ref=recv.at[pl.ds(0, nodes - 1)],
            send_sem=out_sem.at[which],
            recv_sem=in_sem.at[which],
            device_id=(lax.rem(node + 1, nodes), place),
            device_id_type=MESH,
        )

    old_place, old_expert = meta_ref[0:1, :], meta_ref[1:2, :]
    new_place, new_expert = meta_ref[2:3, :], meta_ref[3:4, :]
    slots = meta_ref.shape[1]
    position = iota((tall, slots), 0) // 4
    at_new = equal(position, new_place).astype(BF16)
    own_row = equal(iota((4 * experts, slots), 0) // 4, new_expert).astype(BF16)
    choose = dot_nt(at_new, own_row)
    same = (iota((tall, 4 * experts), 0) % 4) == (iota((tall, 4 * experts), 1) % 4)
    choose = jnp.where(same, choose, 0.0).astype(BF16)
    for a, ref in enumerate((weight_ref, first_ref, second_ref)):
        picked = dot(choose, ref[...].astype(BF16))
        state_send[:, a] = picked.reshape(nodes, 8, LANES).astype(BF16)
    quarter = nodes // 4
    scatter(state_send, state_recv, 0, 1, quarter)
    for c, way in chains:
        advance(c, way, 1)
    scatter(state_send, state_recv, 0, quarter, 2 * quarter)
    state_recv[node] = state_send[node]
    for c, way in chains:
        advance(c, way, 2)
    scatter(state_send, state_recv, 0, 2 * quarter, 3 * quarter)

    at_old = equal(position, old_place).astype(BF16)
    expert = iota((experts, slots), 0)
    held_new = dot_nt(at_new, equal(expert, new_expert).astype(BF16)).astype(BF16)
    held_old = dot_nt(at_old, equal(expert, old_expert).astype(BF16)).astype(BF16)
    pairs = dot_nt(held_new, held_old)
    tall_row, tall_column = iota((tall, tall), 0), iota((tall, tall), 1)
    match[...] = jnp.where((tall_row % 4) == (tall_column % 4), pairs, 0.0).astype(BF16)
    q, r = tall_row // rows, tall_row % rows
    order[...] = equal(tall_column, (r // 2) * 8 + q * 2 + r % 2).astype(BF16)
    for k in range(3, half):
        for c, way in chains:
            advance(c, way, k)
    scatter(state_send, state_recv, 0, 3 * quarter, nodes)

    for c in range(2):
        value = partial(c, 0)
        for way in (1, -1):
            k = chains[(c, way)] - 1
            hop(c, way, k).wait_recv()
            value = value + ring_recv[slot[(c, way, k)]].astype(F32)
        for h in range(2):
            total[pl.ds((2 * c + h) * rows, rows), :] = value[:, h * LANES : (h + 1) * LANES].astype(BF16)
    mine = lax.dot_general(
        order[...], total[...], (((0,), (0,)), ((), ())), preferred_element_type=F32
    )
    rows_send[...] = mine.reshape(nodes, 8, LANES).astype(BF16)
    scatter(rows_send, rows_recv, 1, 1, nodes)
    rows_recv[node] = rows_send[node]

    def natural(block, out):
        value = dot(order[...], block.astype(F32).reshape(tall, LANES).astype(BF16))
        for c in range(2):
            for h in range(2):
                out[c, :, h * LANES : (h + 1) * LANES] = value[
                    (2 * c + h) * rows : (2 * c + h + 1) * rows
                ].astype(BF16)

    all_but_one(state_send, state_recv, 0).wait_recv()
    for a, out in enumerate((out_weight, out_first, out_second)):
        natural(state_recv[:, a], out)

    all_but_one(rows_send, rows_recv, 1).wait_recv()
    summed = dot(match[...], rows_recv[...].astype(F32).reshape(tall, LANES).astype(BF16))
    slots_send[...] = summed.reshape(nodes, 8, LANES).astype(BF16)
    scatter(slots_send, slots_recv, 2, 1, nodes)
    slots_recv[node] = slots_send[node]

    for key, length in chains.items():
        for k in range(length):
            hop(*key, k).wait_send()
    all_but_one(state_send, state_recv, 0).wait_send()
    all_but_one(rows_send, rows_recv, 1).wait_send()
    all_but_one(slots_send, slots_recv, 2).wait_recv()
    natural(slots_recv[...], out_grad)
    all_but_one(slots_send, slots_recv, 2).wait_send()


def by_row(state):
    experts = state.shape[0]
    return state.reshape(experts, 2, 2, LANES).transpose(0, 2, 1, 3).reshape(4 * experts, LANES)


def local(
    master_weight,
    first_moment,
    second_moment,
    features,
    grad_out,
    old_place,
    new_place,
    old_owner,
    new_owner,
):
    nodes, ring = lax.axis_size("node"), lax.axis_size("local")
    experts = master_weight.shape[0]
    rows = features.shape[3]
    columns = master_weight.shape[2]
    primaries = jnp.arange(experts, dtype=jnp.int32)
    meta = jnp.stack(
        [
            old_place,
            jnp.concatenate([primaries, old_owner]),
            new_place,
            jnp.concatenate([primaries, new_owner]),
        ]
    )
    tall = 8 * nodes
    hops = 2 * (ring - 1)
    vmem = pl.BlockSpec(memory_space=pltpu.VMEM)
    block = jax.ShapeDtypeStruct((2, rows, columns), BF16)
    weight_old, first_old, second_old, gradient = pl.pallas_call(
        functools.partial(exchange, nodes, ring),
        out_shape=(block,) * 4,
        in_specs=[vmem] * 6,
        out_specs=(vmem,) * 4,
        scratch_shapes=[
            pltpu.VMEM((2, rows, features.shape[2]), BF16),
            pltpu.VMEM((hops, rows, columns), BF16),
            pltpu.VMEM((hops, rows, columns), BF16),
            pltpu.VMEM((nodes, 3, 8, LANES), BF16),
            pltpu.VMEM((nodes, 3, 8, LANES), BF16),
            pltpu.VMEM((nodes, 8, LANES), BF16),
            pltpu.VMEM((nodes, 8, LANES), BF16),
            pltpu.VMEM((nodes, 8, LANES), BF16),
            pltpu.VMEM((nodes, 8, LANES), BF16),
            pltpu.VMEM((tall, LANES), BF16),
            pltpu.VMEM((tall, tall), BF16),
            pltpu.VMEM((tall, tall), BF16),
            pltpu.SemaphoreType.DMA((hops,)),
            pltpu.SemaphoreType.DMA((hops,)),
            pltpu.SemaphoreType.DMA((3,)),
            pltpu.SemaphoreType.DMA((3,)),
        ],
        compiler_params=pltpu.CompilerParams(
            collective_id=0, has_side_effects=True, vmem_limit_bytes=32 * 1024 * 1024
        ),
        name="exchange",
    )(
        meta,
        by_row(master_weight),
        by_row(first_moment),
        by_row(second_moment),
        features.reshape(2, features.shape[2], rows),
        grad_out.reshape(2, grad_out.shape[2], grad_out.shape[3]),
    )
    gradient = gradient.astype(F32)
    first_new = BETA_FIRST * first_old.astype(F32) + (1.0 - BETA_FIRST) * gradient
    second_new = BETA_SECOND * second_old.astype(F32) + (1.0 - BETA_SECOND) * gradient * gradient
    weight_old = weight_old.astype(F32)
    update = (
        first_new / CORRECT_FIRST / (jnp.sqrt(second_new / CORRECT_SECOND) + EPSILON)
        + DECAY_RATE * weight_old
    )
    weight_new = (weight_old - LEARNING_RATE * update).astype(BF16)
    return weight_new, first_new, second_new


def solution(mesh):
    return jax.shard_map(
        local,
        mesh=mesh,
        in_specs=(
            P(None, "node", "local"),
            P(None, "node", "local"),
            P(None, "node", "local"),
            P("node", "local", None, None),
            P("node", "local", None, None),
            P(),
            P(),
            P(),
            P(),
        ),
        out_specs=(P("node", None, "local"), P("node", None, "local"), P("node", None, "local")),
        check_vma=False,
    )
```

time: 162 us -> 56.3 us (0.35)
  waiting for transfers between devices: 88.9 us -> 0 us
  Pallas kernels: 0 us -> 48.2 us
  starting transfers between devices: 41.9 us -> 0 us
  between operations: 14.3 us -> 0.68 us
  local copies, waits for them, and re-layouts: 11.5 us -> 6.02 us
  matrix products: 4.18 us -> 0 us
    all_to_all x4 -> x0, waiting for transfers between devices: 57.6 us -> none  [the longest x1 28 us: local(): lax.all_to_all(slot_grad.reshape(capacity, node_count, block_rows, hidden...]
    pallas_call x0 -> x1, Pallas kernels: none -> 48.2 us  [local(): pl.pallas_call(functools.partial(exchange, nodes, ring), out_shape=(block...]
    all_to_all x4 -> x0, starting transfers between devices: 41.9 us -> none  [the longest x1 16 us: local(): lax.all_to_all(send_weight.reshape(capacity, node_count, block_rows, colu...]
    reduce_scatter x1 -> x0, waiting for transfers between devices: 31.2 us -> none  [local(): lax.psum_scatter(summed.reshape(experts, block_rows, hidden_width).astype...]
    reshape x12 -> x0, local copies, waits for them, and re-layouts: 4.34 us -> none  [the longest x2 1.39 us: local(): blocks.reshape(capacity, node_count, block_rows * hidden_width)]
    dot_general x7 -> x0, matrix products: 4.18 us -> none  [the longest x1 1.43 us: local(): jnp.einsum('ekc,ckx->ex', collect, blocks.reshape(capacity, node_count, b...]
    convert_element_type x4 -> x0, local copies, waits for them, and re-layouts: 3.11 us -> none  [the longest x2 2.93 us: local(): slot_grad.reshape(capacity, node_count, block_rows, hidden_width)]
    unnamed x19 -> x18, local copies, waits for them, and re-layouts: 3.37 us -> 6.02 us
  transfers between devices with their start and end apart: 5 -> 0, of which waited for: 5 -> 0; matrix products, arithmetic and copies ran while one was open for 3% -> 0% of each run, Pallas kernels for 0% -> 0%
where the time goes in v1:
time: 56.3 us; the launch traced here: 55.9 us
  Pallas kernels  48.2 us (86%)
  local copies, waits for them, and re-layouts  6.02 us (11%)
  other arithmetic  1.07 us (2%)
  between operations  0.68 us (1%)
    pallas_call x1, Pallas kernels, local(): pl.pallas_call(functools.partial(exchange, nodes, ring), out_shape=(block...  48.2 us
    unnamed x18, local copies, waits for them, and re-layouts  6.02 us

profile of v1, /device:TPU:1, one launch (start us, length us, event | category | flops | bytes accessed | tf_op | source)
XLA Modules:
  0.0 55.9 jit_solution(4541897372633269306)
XLA Ops:
  0.6 0.0 copy-start.5
  0.6 0.0 copy-start.6
  0.7 0.6 %copy-done.5 = s32[16]{0:T(128)S(1)} copy-done((s32[16]{0:T(128)S(1)}, s32[16]{0:T(128)}, u32[]{:S(2)}) %copy-start.5) | copy-done | bytes 88
  1.3 0.0 copy-done.6
  1.3 0.1 add_bitcast_fusion
  1.4 0.0 copy-start.7
  1.4 0.0 copy-start.8
  1.4 0.7 %copy-done.7 = s32[80]{0:T(128)S(1)} copy-done((s32[80]{0:T(128)S(1)}, s32[80]{0:T(128)}, u32[]{:S(2)}) %copy-start.7) | copy-done | bytes 344
  2.0 0.0 copy-done.8
  2.1 0.0 copy-start
  2.1 1.2 %copy-done = bf16[2,1,128,2048]{3,2,1,0:T(8,128)(2,1)S(1)} copy-done((bf16[2,1,128,2048]{3,2,1,0:T(8,128)(2,1)S(1)}, bf16[2,1,128,2048]{3,2,1,0:T(8,128)(2,1)}, u32[]{:S(2)}) %copy-start) | copy-done | bytes 1048600
  3.3 0.0 copy-start.1
  3.3 0.9 %copy-done.1 = f32[64,2,256]{2,1,0:T(2,128)S(1)} copy-done((f32[64,2,256]{2,1,0:T(2,128)S(1)}, f32[64,2,256]{2,1,0:T(2,128)}, u32[]{:S(2)}) %copy-start.1) | copy-done | bytes 131096
  4.2 0.0 copy-start.2
  4.2 0.9 %copy-done.2 = f32[64,2,256]{2,1,0:T(2,128)S(1)} copy-done((f32[64,2,256]{2,1,0:T(2,128)S(1)}, f32[64,2,256]{2,1,0:T(2,128)}, u32[]{:S(2)}) %copy-start.2) | copy-done | bytes 131096
  5.1 0.0 copy-start.3
  5.1 0.8 %copy-done.3 = bf16[64,2,256]{2,1,0:T(2,128)(2,1)S(1)} copy-done((bf16[64,2,256]{2,1,0:T(2,128)(2,1)S(1)}, bf16[64,2,256]{2,1,0:T(2,128)(2,1)}, u32[]{:S(2)}) %copy-start.3) | copy-done | bytes 65560
  5.9 0.0 copy-start.4
  5.9 0.8 %copy-done.4 = bf16[2,1,128,128]{3,2,1,0:T(8,128)(2,1)S(1)} copy-done((bf16[2,1,128,128]{3,2,1,0:T(8,128)(2,1)S(1)}, bf16[2,1,128,128]{3,2,1,0:T(8,128)(2,1)}, u32[]{:S(2)}) %copy-start.4) | copy-done | bytes 65560
  6.8 48.2 %exchange.1 = (bf16[2,128,256]{2,1,0:T(8,128)(2,1)S(1)}, bf16[2,128,256]{2,1,0:T(8,128)(2,1)S(1)}, bf16[2,128,256]{2,1,0:T(8,128)(2,1)S(1)}, bf16[2,128,256]{2,1,0:T(8,128)(2,1)S(1)}) custom-call(s32[4,80]{1,0:T(4,128)S(1)} %pad_add_fusion.meta_ref, bf16[256,128]{1,0:T(8,128)(2,1)S(1)} %bitcast.26, f32[256,128]{1,0:T(8,128)S(1)} %bitcast.24, ...), custom_call_target="tpu_custom_call" | custom-call | tf_op jit(solution)/shard_map/exchange/pallas_call | solution.py:271
  55.0 1.0 %fusion.2 = (bf16[2,128,256]{2,1,0:T(8,128)(2,1)}, f32[2,128,256]{2,1,0:T(8,128)}, f32[2,128,256]{2,1,0:T(8,128)}) fusion(bf16[2,128,256]{2,1,0:T(8,128)(2,1)S(1)} %get-tuple-element.7, bf16[2,128,256]{2,1,0:T(8,128)(2,1)S(1)} %get-tuple-element.9, bf16[2,128,256]{2,1,0:T(8,128)(2,1)S(1)} %get-tuple-element.8, bf16[2,128,256]{2,1,0:T(8,128)(2,1)S(1)} %get-tuple-element.10), kind=kLoop, calls=%fused_computation.6 | loop fusion | flops 1310720 | bytes 1179648 | tf_op jit(solution)/shard_map/convert_element_type | solution.py:314
  (2 shorter events, 0.0 us)
Async XLA Ops:
  0.6 0.7 %copy-start.5 = (s32[16]{0:T(128)S(1)}, s32[16]{0:T(128)}, u32[]{:S(2)}) copy-start(s32[16]{0:T(128)} %param.16) | copy-start | bytes 196
  0.6 0.7 %copy-start.6 = (s32[16]{0:T(128)S(1)}, s32[16]{0:T(128)}, u32[]{:S(2)}) copy-start(s32[16]{0:T(128)} %param.17) | copy-start | bytes 196
  1.4 0.7 %copy-start.7 = (s32[80]{0:T(128)S(1)}, s32[80]{0:T(128)}, u32[]{:S(2)}) copy-start(s32[80]{0:T(128)} %param.15) | copy-start | bytes 964
  1.4 0.7 %copy-start.8 = (s32[80]{0:T(128)S(1)}, s32[80]{0:T(128)}, u32[]{:S(2)}) copy-start(s32[80]{0:T(128)} %param.14) | copy-start | bytes 964
  2.1 1.2 %copy-start = (bf16[2,1,128,2048]{3,2,1,0:T(8,128)(2,1)S(1)}, bf16[2,1,128,2048]{3,2,1,0:T(8,128)(2,1)}, u32[]{:S(2)}) copy-start(bf16[2,1,128,2048]{3,2,1,0:T(8,128)(2,1)} %param.13) | copy-start | bytes 3145732
  3.3 0.9 %copy-start.1 = (f32[64,2,256]{2,1,0:T(2,128)S(1)}, f32[64,2,256]{2,1,0:T(2,128)}, u32[]{:S(2)}) copy-start(f32[64,2,256]{2,1,0:T(2,128)} %param.10) | copy-start | bytes 393220
  4.2 0.9 %copy-start.2 = (f32[64,2,256]{2,1,0:T(2,128)S(1)}, f32[64,2,256]{2,1,0:T(2,128)}, u32[]{:S(2)}) copy-start(f32[64,2,256]{2,1,0:T(2,128)} %param.11) | copy-start | bytes 393220
  5.1 0.8 %copy-start.3 = (bf16[64,2,256]{2,1,0:T(2,128)(2,1)S(1)}, bf16[64,2,256]{2,1,0:T(2,128)(2,1)}, u32[]{:S(2)}) copy-start(bf16[64,2,256]{2,1,0:T(2,128)(2,1)} %param.9) | copy-start | bytes 196612
  5.9 0.8 %copy-start.4 = (bf16[2,1,128,128]{3,2,1,0:T(8,128)(2,1)S(1)}, bf16[2,1,128,128]{3,2,1,0:T(8,128)(2,1)}, u32[]{:S(2)}) copy-start(bf16[2,1,128,128]{3,2,1,0:T(8,128)(2,1)} %param.12) | copy-start | bytes 196612

commit v2 on v1

v2 whole, which is shorter than its diff:
```python
import functools

import jax
import jax.numpy as jnp
from jax import lax
from jax.experimental import pallas as pl
from jax.experimental.pallas import tpu as pltpu
from jax.sharding import PartitionSpec as P

BETA_FIRST = 0.9
BETA_SECOND = 0.95
LEARNING_RATE = 0.1
DECAY_RATE = 0.1
EPSILON = 1e-08
CORRECT_FIRST = 1.0 - 0.9**10
CORRECT_SECOND = 1.0 - 0.95**10

MESH = pl.DeviceIdType.MESH
LANES = 128
CHUNKS = 4
F32 = jnp.float32
BF16 = jnp.bfloat16


def dot(a, b):
    return jnp.dot(a, b, preferred_element_type=F32)


def dot_nt(a, b):
    return lax.dot_general(a, b, (((1,), (1,)), ((), ())), preferred_element_type=F32)


def equal(a, b):
    return jnp.where(a == b, 1.0, 0.0)


def iota(shape, axis):
    return lax.broadcasted_iota(jnp.int32, shape, axis)


def exchange(
    nodes,
    ring,
    old_place_hbm,
    new_place_hbm,
    old_owner_hbm,
    new_owner_hbm,
    weight_hbm,
    first_hbm,
    second_hbm,
    features_hbm,
    grad_hbm,
    out_weight,
    out_first,
    out_second,
    out_grad,
    old_place_ref,
    new_place_ref,
    old_owner_ref,
    new_owner_ref,
    weight_ref,
    first_ref,
    second_ref,
    features_ref,
    grad_ref,
    load_sem,
    turned,
    ring_send,
    ring_recv,
    state_send,
    state_recv,
    rows_send,
    rows_recv,
    slots_send,
    slots_recv,
    parts,
    total,
    piece_order,
    order,
    match,
    ring_out_sem,
    ring_in_sem,
    out_sem,
    in_sem,
):
    node = lax.axis_index("node")
    place = lax.axis_index("local")
    experts = weight_ref.shape[0] // 4
    rows = features_ref.shape[2]
    columns = 2 * LANES
    tall = 8 * nodes
    half = ring // 2
    loads = [
        pltpu.make_async_copy(source, target, load_sem.at[i])
        for i, (source, target) in enumerate(
            (
                (features_hbm, features_ref),
                (grad_hbm, grad_ref),
                (new_place_hbm, new_place_ref),
                (new_owner_hbm, new_owner_ref),
                (weight_hbm, weight_ref),
                (first_hbm, first_ref),
                (second_hbm, second_ref),
                (old_place_hbm, old_place_ref),
                (old_owner_hbm, old_owner_ref),
            )
        )
    ]

    barrier = pltpu.get_barrier_semaphore()

    def greet(k, carry):
        pl.semaphore_signal(
            barrier, inc=1, device_id=(lax.rem(node + k, nodes), place), device_id_type=MESH
        )
        return carry

    lax.fori_loop(1, nodes, greet, 0)
    right = lax.rem(place + 1, ring)
    left = lax.rem(place + ring - 1, ring)
    for neighbour in (right, left):
        pl.semaphore_signal(barrier, inc=1, device_id=(node, neighbour), device_id_type=MESH)

    for load in loads:
        load.start()
    for load in loads[:2]:
        load.wait()
    for c in range(2):
        turned[c] = features_ref[c].astype(F32).T.astype(BF16)

    def partial(c, ahead):
        block = lax.rem(place + ahead + ring, ring)
        at = pl.multiple_of(block * columns, columns)
        return dot(turned[c], grad_ref[c, :, pl.ds(at, columns)])

    chains = {(0, 1): half, (1, -1): half, (0, -1): half - 1, (1, 1): half - 1}
    slot = {}
    for key, length in chains.items():
        for k in range(length):
            slot[key + (k,)] = len(slot)
    piece = rows // CHUNKS

    def hop(c, way, k, j):
        at = slot[(c, way, k)]
        return pltpu.make_async_remote_copy(
            src_ref=ring_send.at[j, at],
            dst_ref=ring_recv.at[j, at],
            send_sem=ring_out_sem.at[j, at],
            recv_sem=ring_in_sem.at[j, at],
            device_id=(node, right if way == 1 else left),
            device_id_type=MESH,
        )

    def advance(c, way, k, j):
        at = slot[(c, way, k)]
        hop(c, way, k - 1, j).wait_recv()
        value = parts[at, pl.ds(j * piece, piece), :] + ring_recv[j, slot[(c, way, k - 1)]].astype(F32)
        ring_send[j, at] = value.astype(BF16)
        hop(c, way, k, j).start()

    for c, way in chains:
        value = partial(c, way * chains[(c, way)]).astype(BF16)
        for j in range(CHUNKS):
            ring_send[j, slot[(c, way, 0)]] = value[j * piece : (j + 1) * piece]
    pl.semaphore_wait(barrier, nodes + 1)
    for j in range(CHUNKS):
        for c, way in chains:
            hop(c, way, 0, j).start()
    for (c, way, k), at in slot.items():
        if k:
            parts[at] = partial(c, way * (chains[(c, way)] - k))
    for c in range(2):
        parts[slot[(c, 1, 0)]] = partial(c, 0)

    def scatter(send, recv, which, first, last):
        def one(k, carry):
            other = lax.rem(node + k, nodes)
            pltpu.make_async_remote_copy(
                src_ref=send.at[other],
                dst_ref=recv.at[node],
                send_sem=out_sem.at[which],
                recv_sem=in_sem.at[which],
                device_id=(other, place),
                device_id_type=MESH,
            ).start()
            return carry

        lax.fori_loop(first, last, one, 0)

    def all_but_one(send, recv, which):
        return pltpu.make_async_remote_copy(
            src_ref=send.at[pl.ds(0, nodes - 1)],
            dst_ref=recv.at[pl.ds(0, nodes - 1)],
            send_sem=out_sem.at[which],
            recv_sem=in_sem.at[which],
            device_id=(lax.rem(node + 1, nodes), place),
            device_id_type=MESH,
        )

    for load in loads[2:]:
        load.wait()
    redundant = old_owner_ref.shape[1]
    slots = experts + redundant
    position = iota((tall, slots), 0) // 4

    def expert_of_slot(owner, repeat):
        owned = equal(iota((experts * repeat, redundant), 0) // repeat, owner).astype(BF16)
        tail = equal(iota((redundant, slots), 0) + experts, iota((redundant, slots), 1)).astype(BF16)
        primary = equal(iota((experts * repeat, slots), 0) // repeat, iota((experts * repeat, slots), 1))
        return (dot(owned, tail) + primary).astype(BF16)

    at_new = equal(position, new_place_ref[...]).astype(BF16)
    choose = dot_nt(at_new, expert_of_slot(new_owner_ref[...], 4))
    same = (iota((tall, 4 * experts), 0) % 4) == (iota((tall, 4 * experts), 1) % 4)
    choose = jnp.where(same, choose, 0.0).astype(BF16)
    for a, ref in enumerate((weight_ref, first_ref, second_ref)):
        picked = dot(choose, ref[...].astype(BF16))
        state_send[:, a] = picked.reshape(nodes, 8, LANES).astype(BF16)
    state_recv[node] = state_send[node]
    steps = (half - 1) * CHUNKS
    bounds = [1 + (nodes - 1) * i // steps for i in range(steps + 1)]
    for k in range(1, half):
        for j in range(CHUNKS):
            for c, way in chains:
                if k < chains[(c, way)]:
                    advance(c, way, k, j)
            i = (k - 1) * CHUNKS + j
            scatter(state_send, state_recv, 0, bounds[i], bounds[i + 1])
        if k == 1:
            at_old = equal(position, old_place_ref[...]).astype(BF16)
            held_new = dot_nt(at_new, expert_of_slot(new_owner_ref[...], 1)).astype(BF16)
            held_old = dot_nt(at_old, expert_of_slot(old_owner_ref[...], 1)).astype(BF16)
            pairs = dot_nt(held_new, held_old)
            tall_row, tall_column = iota((tall, tall), 0), iota((tall, tall), 1)
            match[...] = jnp.where((tall_row % 4) == (tall_column % 4), pairs, 0.0).astype(BF16)
        if k == 2:
            q, r = tall_row // rows, tall_row % rows
            order[0] = equal(tall_column, (r // 2) * 8 + q * 2 + r % 2).astype(BF16)
            owner = (r % piece) // 2 * CHUNKS + r // piece
            order[1] = equal(tall_column, owner * 8 + q * 2 + r % 2).astype(BF16)
            short = 4 * piece
            short_row, short_column = iota((short, short), 0), iota((short, short), 1)
            q, r = short_column // piece, short_column % piece
            piece_order[...] = equal(short_row, (r // 2) * 8 + q * 2 + r % 2).astype(BF16)

    group = nodes // CHUNKS
    for j in range(CHUNKS):
        for c in range(2):
            value = parts[slot[(c, 1, 0)], pl.ds(j * piece, piece), :]
            for way in (1, -1):
                k = chains[(c, way)] - 1
                hop(c, way, k, j).wait_recv()
                value = value + ring_recv[j, slot[(c, way, k)]].astype(F32)
            value = value.astype(BF16)
            for h in range(2):
                total[j, pl.ds((2 * c + h) * piece, piece), :] = value[:, h * LANES : (h + 1) * LANES]
        mine = dot(piece_order[...], total[j])
        rows_send[j] = mine.reshape(group, 8, LANES).astype(BF16)

        def give(k, carry, j=j):
            at = lax.rem(node // CHUNKS + k, group)
            pltpu.make_async_remote_copy(
                src_ref=rows_send.at[j, at],
                dst_ref=rows_recv.at[node],
                send_sem=out_sem.at[1],
                recv_sem=in_sem.at[1],
                device_id=(at * CHUNKS + j, place),
                device_id_type=MESH,
            ).start()
            return carry

        lax.fori_loop(1, group, give, 0)

        @pl.when(lax.rem(node, CHUNKS) != j)
        def _(give=give):
            give(0, 0)

    rows_recv[node] = rows_send[lax.rem(node, CHUNKS), node // CHUNKS]

    def natural(block, out, which):
        value = dot(order[which], block.astype(F32).reshape(tall, LANES).astype(BF16))
        for c in range(2):
            for h in range(2):
                out[c, :, h * LANES : (h + 1) * LANES] = value[
                    (2 * c + h) * rows : (2 * c + h + 1) * rows
                ].astype(BF16)

    all_but_one(state_send, state_recv, 0).wait_recv()
    for a, out in enumerate((out_weight, out_first, out_second)):
        natural(state_recv[:, a], out, 0)

    all_but_one(rows_recv, rows_recv, 1).wait_recv()
    summed = dot(match[...], rows_recv[...].astype(F32).reshape(tall, LANES).astype(BF16))
    slots_send[...] = summed.reshape(nodes, 8, LANES).astype(BF16)
    scatter(slots_send, slots_recv, 2, 1, nodes)
    slots_recv[node] = slots_send[node]

    for key, length in chains.items():
        for k in range(length):
            for j in range(CHUNKS):
                hop(*key, k, j).wait_send()
    all_but_one(state_send, state_recv, 0).wait_send()
    all_but_one(rows_recv, rows_recv, 1).wait_send()
    all_but_one(slots_send, slots_recv, 2).wait_recv()
    natural(slots_recv[...], out_grad, 1)
    all_but_one(slots_send, slots_recv, 2).wait_send()


def by_row(state):
    experts = state.shape[0]
    return state.reshape(experts, 2, 2, LANES).transpose(0, 2, 1, 3).reshape(4 * experts, LANES)


def local(
    master_weight,
    first_moment,
    second_moment,
    features,
    grad_out,
    old_place,
    new_place,
    old_owner,
    new_owner,
):
    nodes, ring = lax.axis_size("node"), lax.axis_size("local")
    experts = master_weight.shape[0]
    rows = features.shape[3]
    columns = master_weight.shape[2]
    tall = 8 * nodes
    hops = 2 * (ring - 1)
    piece = rows // CHUNKS
    operands = (
        old_place.reshape(1, -1),
        new_place.reshape(1, -1),
        old_owner.reshape(1, -1),
        new_owner.reshape(1, -1),
        by_row(master_weight),
        by_row(first_moment),
        by_row(second_moment),
        features.reshape(2, features.shape[2], rows),
        grad_out.reshape(2, grad_out.shape[2], grad_out.shape[3]),
    )
    vmem = pl.BlockSpec(memory_space=pltpu.VMEM)
    block = jax.ShapeDtypeStruct((2, rows, columns), BF16)
    weight_old, first_old, second_old, gradient = pl.pallas_call(
        functools.partial(exchange, nodes, ring),
        out_shape=(block,) * 4,
        in_specs=[pl.BlockSpec(memory_space=pltpu.HBM)] * len(operands),
        out_specs=(vmem,) * 4,
        scratch_shapes=[
            *(pltpu.VMEM(operand.shape, operand.dtype) for operand in operands),
            pltpu.SemaphoreType.DMA((len(operands),)),
            pltpu.VMEM((2, rows, features.shape[2]), BF16),
            pltpu.VMEM((CHUNKS, hops, piece, columns), BF16),
            pltpu.VMEM((CHUNKS, hops, piece, columns), BF16),
            pltpu.VMEM((nodes, 3, 8, LANES), BF16),
            pltpu.VMEM((nodes, 3, 8, LANES), BF16),
            pltpu.VMEM((CHUNKS, nodes // CHUNKS, 8, LANES), BF16),
            pltpu.VMEM((nodes, 8, LANES), BF16),
            pltpu.VMEM((nodes, 8, LANES), BF16),
            pltpu.VMEM((nodes, 8, LANES), BF16),
            pltpu.VMEM((hops, rows, columns), F32),
            pltpu.VMEM((CHUNKS, 4 * piece, LANES), BF16),
            pltpu.VMEM((4 * piece, 4 * piece), BF16),
            pltpu.VMEM((2, tall, tall), BF16),
            pltpu.VMEM((tall, tall), BF16),
            pltpu.SemaphoreType.DMA((CHUNKS, hops)),
            pltpu.SemaphoreType.DMA((CHUNKS, hops)),
            pltpu.SemaphoreType.DMA((3,)),
            pltpu.SemaphoreType.DMA((3,)),
        ],
        compiler_params=pltpu.CompilerParams(
            collective_id=0, has_side_effects=True, vmem_limit_bytes=60 * 1024 * 1024
        ),
        name="exchange",
    )(*operands)
    gradient = gradient.astype(F32)
    first_new = BETA_FIRST * first_old.astype(F32) + (1.0 - BETA_FIRST) * gradient
    second_new = BETA_SECOND * second_old.astype(F32) + (1.0 - BETA_SECOND) * gradient * gradient
    weight_old = weight_old.astype(F32)
    update = (
        first_new / CORRECT_FIRST / (jnp.sqrt(second_new / CORRECT_SECOND) + EPSILON)
        + DECAY_RATE * weight_old
    )
    weight_new = (weight_old - LEARNING_RATE * update).astype(BF16)
    return weight_new, first_new, second_new


def solution(mesh):
    return jax.shard_map(
        local,
        mesh=mesh,
        in_specs=(
            P(None, "node", "local"),
            P(None, "node", "local"),
            P(None, "node", "local"),
            P("node", "local", None, None),
            P("node", "local", None, None),
            P(),
            P(),
            P(),
            P(),
        ),
        out_specs=(P("node", None, "local"), P("node", None, "local"), P("node", None, "local")),
        check_vma=False,
    )
```

time: 56.3 us -> 48.3 us (0.86)
  local copies, waits for them, and re-layouts: 6.02 us -> 0 us
  Pallas kernels: 48.2 us -> 45.4 us
  other arithmetic: 1.07 us -> 2.08 us
    unnamed x18 -> x0, local copies, waits for them, and re-layouts: 6.02 us -> none
    pallas_call x1, Pallas kernels: 48.2 us -> 45.4 us  [local(): pl.pallas_call(functools.partial(exchange, nodes, ring), out_shape=(block...]
    convert_element_type x1, other arithmetic: 0.99 us -> 2.08 us  [local(): weight_new = (weight_old - LEARNING_RATE * update).astype(BF16)]
where the time goes in v2:
time: 48.3 us; the launch traced here: 48.2 us
  Pallas kernels  45.4 us (94%)
  other arithmetic  2.08 us (4%)
  between operations  0.64 us (1%)
    pallas_call x1, Pallas kernels, local(): pl.pallas_call(functools.partial(exchange, nodes, ring), out_shape=(block...  45.4 us
    convert_element_type x1, other arithmetic, local(): weight_new = (weight_old - LEARNING_RATE * update).astype(BF16)  2.08 us

profile of v2, /device:TPU:1, one launch (start us, length us, event | category | flops | bytes accessed | tf_op | source)
XLA Modules:
  0.0 48.2 jit_solution(4193483532824199372)
XLA Ops:
  0.6 45.4 %exchange.1 = (bf16[2,128,256]{2,1,0:T(8,128)(2,1)}, bf16[2,128,256]{2,1,0:T(8,128)(2,1)}, bf16[2,128,256]{2,1,0:T(8,128)(2,1)}, bf16[2,128,256]{2,1,0:T(8,128)(2,1)}) custom-call(s32[1,80]{1,0:T(1,128)} %bitcast.26, s32[1,80]{1,0:T(1,128)} %bitcast.27, s32[1,16]{1,0:T(1,128)} %bitcast.28, s32[1,16]{1,0:T(1,128)} %bitcast.29, bf16[256,128]{1,0:T(8,128)(2,1)} %bitcast.24, ...), custom_call_target="tpu_custom_call" | custom-call | tf_op jit(solution)/shard_map/exchange/pallas_call | solution.py:345
  46.1 2.1 %fusion.2 = (bf16[2,128,256]{2,1,0:T(8,128)(2,1)}, f32[2,128,256]{2,1,0:T(8,128)}, f32[2,128,256]{2,1,0:T(8,128)}) fusion(bf16[2,128,256]{2,1,0:T(8,128)(2,1)} %get-tuple-element.7, bf16[2,128,256]{2,1,0:T(8,128)(2,1)} %get-tuple-element.9, bf16[2,128,256]{2,1,0:T(8,128)(2,1)} %get-tuple-element.8, bf16[2,128,256]{2,1,0:T(8,128)(2,1)} %get-tuple-element.10), kind=kLoop, calls=%fused_computation.6 | loop fusion | flops 1310720 | bytes 1179648 | tf_op jit(solution)/shard_map/convert_element_type | solution.py:385

commit v3 on v2

--- a/solution.py
+++ b/solution.py
@@ -18,6 +18,7 @@
 MESH = pl.DeviceIdType.MESH
 LANES = 128
 CHUNKS = 4
+CHIPS_X, CHIPS_Z = 4, 8
 F32 = jnp.float32
 BF16 = jnp.bfloat16
 
@@ -82,6 +83,7 @@
     ring_in_sem,
     out_sem,
     in_sem,
+    round_sem,
 ):
     node = lax.axis_index("node")
     place = lax.axis_index("local")
@@ -107,19 +109,39 @@
         )
     ]
 
+    x, z, core = node // (2 * CHIPS_Z), lax.rem(node // 2, CHIPS_Z), lax.rem(node, 2)
+
+    def away(dx, dz, dc):
+        to_x = lax.rem(x + dx, CHIPS_X) if dx else x
+        to_z = lax.rem(z + dz, CHIPS_Z) if dz else z
+        return (to_x * CHIPS_Z + to_z) * 2 + (1 - core if dc else core)
+
+    def distance(offset):
+        dx, dz = offset[0], offset[1]
+        return min(dx, CHIPS_X - dx) + min(dz, CHIPS_Z - dz)
+
+    offsets = [(dx, dz, dc) for dx in range(CHIPS_X) for dz in range(CHIPS_Z) for dc in range(2)][1:]
+    offsets.sort(key=distance, reverse=True)
+    farthest = distance(offsets[0])
+    next_to = [(1, 0), (CHIPS_X - 1, 0), (0, 1), (0, CHIPS_Z - 1)]
+
     barrier = pltpu.get_barrier_semaphore()
-
-    def greet(k, carry):
-        pl.semaphore_signal(
-            barrier, inc=1, device_id=(lax.rem(node + k, nodes), place), device_id_type=MESH
-        )
-        return carry
-
-    lax.fori_loop(1, nodes, greet, 0)
     right = lax.rem(place + 1, ring)
     left = lax.rem(place + ring - 1, ring)
     for neighbour in (right, left):
         pl.semaphore_signal(barrier, inc=1, device_id=(node, neighbour), device_id_type=MESH)
+    close = [(0, 0, 1)] + [(dx, dz, dc) for dx, dz in next_to for dc in range(2)]
+    for offset in close:
+        pl.semaphore_signal(barrier, inc=1, device_id=(away(*offset), place), device_id_type=MESH)
+
+    def tell(r):
+        for dx, dz in next_to:
+            pl.semaphore_signal(
+                round_sem.at[r - 1], inc=1, device_id=(away(dx, dz, 0), place), device_id_type=MESH
+            )
+
+    def hear(r):
+        pl.semaphore_wait(round_sem.at[r - 1], len(next_to))
 
     for load in loads:
         load.start()
@@ -162,19 +184,20 @@
         value = partial(c, way * chains[(c, way)]).astype(BF16)
         for j in range(CHUNKS):
             ring_send[j, slot[(c, way, 0)]] = value[j * piece : (j + 1) * piece]
-    pl.semaphore_wait(barrier, nodes + 1)
+    pl.semaphore_wait(barrier, 2 + len(close))
     for j in range(CHUNKS):
         for c, way in chains:
             hop(c, way, 0, j).start()
+    tell(1)
     for (c, way, k), at in slot.items():
         if k:
             parts[at] = partial(c, way * (chains[(c, way)] - k))
     for c in range(2):
         parts[slot[(c, 1, 0)]] = partial(c, 0)
 
-    def scatter(send, recv, which, first, last):
-        def one(k, carry):
-            other = lax.rem(node + k, nodes)
+    def scatter(send, recv, which, some):
+        for offset in some:
+            other = away(*offset)
             pltpu.make_async_remote_copy(
                 src_ref=send.at[other],
                 dst_ref=recv.at[node],
@@ -183,9 +206,9 @@
                 device_id=(other, place),
                 device_id_type=MESH,
             ).start()
-            return carry
-
-        lax.fori_loop(first, last, one, 0)
+
+    def state_up_to(low, high):
+        scatter(state_send, state_recv, 0, [o for o in offsets if low <= distance(o) <= high])
 
     def all_but_one(send, recv, which):
         return pltpu.make_async_remote_copy(
@@ -217,15 +240,21 @@
         picked = dot(choose, ref[...].astype(BF16))
         state_send[:, a] = picked.reshape(nodes, 8, LANES).astype(BF16)
     state_recv[node] = state_send[node]
-    steps = (half - 1) * CHUNKS
-    bounds = [1 + (nodes - 1) * i // steps for i in range(steps + 1)]
+    state_up_to(0, 1)
+    last_step = (half - 1) * CHUNKS - 1
+    heard = 0
     for k in range(1, half):
         for j in range(CHUNKS):
             for c, way in chains:
                 if k < chains[(c, way)]:
                     advance(c, way, k, j)
-            i = (k - 1) * CHUNKS + j
-            scatter(state_send, state_recv, 0, bounds[i], bounds[i + 1])
+            due = ((k - 1) * CHUNKS + j + 1) * (farthest - 1) // (last_step + 1)
+            while heard < due:
+                heard += 1
+                hear(heard)
+                if heard < farthest - 1:
+                    tell(heard + 1)
+                state_up_to(heard + 1, heard + 1)
         if k == 1:
             at_old = equal(position, old_place_ref[...]).astype(BF16)
             held_new = dot_nt(at_new, expert_of_slot(new_owner_ref[...], 1)).astype(BF16)
@@ -244,6 +273,19 @@
             piece_order[...] = equal(short_row, (r // 2) * 8 + q * 2 + r % 2).astype(BF16)
 
     group = nodes // CHUNKS
+    line = group // CHIPS_X
+    steps = sorted(
+        range(group),
+        key=lambda k: -distance((k // line, k % line * CHIPS_Z // line)),
+    )
+    hosts = [
+        (
+            k,
+            lax.rem(node // (line * CHUNKS) + k // line, CHIPS_X) * line
+            + lax.rem(node // CHUNKS + k % line, line),
+        )
+        for k in steps
+    ]
     for j in range(CHUNKS):
         for c in range(2):
             value = parts[slot[(c, 1, 0)], pl.ds(j * piece, piece), :]
@@ -257,23 +299,19 @@
         mine = dot(piece_order[...], total[j])
         rows_send[j] = mine.reshape(group, 8, LANES).astype(BF16)
 
-        def give(k, carry, j=j):
-            at = lax.rem(node // CHUNKS + k, group)
-            pltpu.make_async_remote_copy(
+        for step, at in hosts:
+            copy = pltpu.make_async_remote_copy(
                 src_ref=rows_send.at[j, at],
                 dst_ref=rows_recv.at[node],
                 send_sem=out_sem.at[1],
                 recv_sem=in_sem.at[1],
                 device_id=(at * CHUNKS + j, place),
                 device_id_type=MESH,
-            ).start()
-            return carry
-
-        lax.fori_loop(1, group, give, 0)
-
-        @pl.when(lax.rem(node, CHUNKS) != j)
-        def _(give=give):
-            give(0, 0)
+            )
+            if step:
+                copy.start()
+            else:
+                pl.when(lax.rem(node, CHUNKS) != j)(copy.start)
 
     rows_recv[node] = rows_send[lax.rem(node, CHUNKS), node // CHUNKS]
 
@@ -292,7 +330,7 @@
     all_but_one(rows_recv, rows_recv, 1).wait_recv()
     summed = dot(match[...], rows_recv[...].astype(F32).reshape(tall, LANES).astype(BF16))
     slots_send[...] = summed.reshape(nodes, 8, LANES).astype(BF16)
-    scatter(slots_send, slots_recv, 2, 1, nodes)
+    scatter(slots_send, slots_recv, 2, offsets)
     slots_recv[node] = slots_send[node]
 
     for key, length in chains.items():
@@ -368,6 +406,7 @@
             pltpu.SemaphoreType.DMA((CHUNKS, hops)),
             pltpu.SemaphoreType.DMA((3,)),
             pltpu.SemaphoreType.DMA((3,)),
+            pltpu.SemaphoreType.REGULAR((CHIPS_X // 2 + CHIPS_Z // 2 - 1,)),
         ],
         compiler_params=pltpu.CompilerParams(
             collective_id=0, has_side_effects=True, vmem_limit_bytes=60 * 1024 * 1024

time: 48.3 us -> 45.9 us (0.950)
  Pallas kernels: 45.4 us -> 43 us
    pallas_call x1, Pallas kernels: 45.4 us -> 43 us  [local(): pl.pallas_call(functools.partial(exchange, nodes, ring), out_shape=(block...]
where the time goes in v3:
time: 45.9 us; the launch traced here: 45.7 us
  Pallas kernels  43 us (94%)
  other arithmetic  2.08 us (5%)
  between operations  0.64 us (1%)
    pallas_call x1, Pallas kernels, local(): pl.pallas_call(functools.partial(exchange, nodes, ring), out_shape=(block...  43 us
    convert_element_type x1, other arithmetic, local(): weight_new = (weight_old - LEARNING_RATE * update).astype(BF16)  2.08 us

profile of v3, /device:TPU:1, one launch (start us, length us, event | category | flops | bytes accessed | tf_op | source)
XLA Modules:
  0.0 45.7 jit_solution(7064596562911101607)
XLA Ops:
  0.6 43.0 %exchange.1 = (bf16[2,128,256]{2,1,0:T(8,128)(2,1)}, bf16[2,128,256]{2,1,0:T(8,128)(2,1)}, bf16[2,128,256]{2,1,0:T(8,128)(2,1)}, bf16[2,128,256]{2,1,0:T(8,128)(2,1)}) custom-call(s32[1,80]{1,0:T(1,128)} %bitcast.26, s32[1,80]{1,0:T(1,128)} %bitcast.27, s32[1,16]{1,0:T(1,128)} %bitcast.28, s32[1,16]{1,0:T(1,128)} %bitcast.29, bf16[256,128]{1,0:T(8,128)(2,1)} %bitcast.24, ...), custom_call_target="tpu_custom_call" | custom-call | tf_op jit(solution)/shard_map/exchange/pallas_call | solution.py:383
  43.6 2.1 %fusion.2 = (bf16[2,128,256]{2,1,0:T(8,128)(2,1)}, f32[2,128,256]{2,1,0:T(8,128)}, f32[2,128,256]{2,1,0:T(8,128)}) fusion(bf16[2,128,256]{2,1,0:T(8,128)(2,1)} %get-tuple-element.7, bf16[2,128,256]{2,1,0:T(8,128)(2,1)} %get-tuple-element.9, bf16[2,128,256]{2,1,0:T(8,128)(2,1)} %get-tuple-element.8, bf16[2,128,256]{2,1,0:T(8,128)(2,1)} %get-tuple-element.10), kind=kLoop, calls=%fused_computation.6 | loop fusion | flops 1310720 | bytes 1179648 | tf_op jit(solution)/shard_map/convert_element_type | solution.py:424

commit v4 on v3

--- a/solution.py
+++ b/solution.py
@@ -65,6 +65,9 @@
     features_ref,
     grad_ref,
     load_sem,
+    block_sem,
+    store_sem,
+    ready,
     turned,
     ring_send,
     ring_recv,
@@ -97,7 +100,6 @@
         for i, (source, target) in enumerate(
             (
                 (features_hbm, features_ref),
-                (grad_hbm, grad_ref),
                 (new_place_hbm, new_place_ref),
                 (new_owner_hbm, new_owner_ref),
                 (weight_hbm, weight_ref),
@@ -143,47 +145,65 @@
     def hear(r):
         pl.semaphore_wait(round_sem.at[r - 1], len(next_to))
 
-    for load in loads:
+    chains = {(0, 1): half, (1, -1): half, (0, -1): half - 1, (1, 1): half - 1}
+    slot = {}
+    for k in range(half):
+        for key, length in chains.items():
+            if k < length:
+                slot[key + (k,)] = len(slot)
+    long = [key for key in chains if chains[key] == half]
+    short = [key for key in chains if chains[key] < half]
+    piece = rows // CHUNKS
+
+    def columns_ahead(ahead):
+        block = lax.rem(place + ahead + ring, ring)
+        return pl.ds(pl.multiple_of(block * columns, columns), columns)
+
+    needs = [(c, way * (chains[(c, way)] - k)) for c, way, k in slot] + [(0, 0), (1, 0)]
+    blocks = {}
+    for i, (c, ahead) in enumerate(needs):
+        at = columns_ahead(ahead)
+        blocks[(c, ahead)] = pltpu.make_async_copy(
+            grad_hbm.at[c, :, at], grad_ref.at[c, :, at], block_sem.at[i]
+        )
+    loads[0].start()
+    for need in needs[: len(chains)]:
+        blocks[need].start()
+    for load in loads[1:]:
         load.start()
-    for load in loads[:2]:
-        load.wait()
+    for need in needs[len(chains) :]:
+        blocks[need].start()
+    loads[0].wait()
     for c in range(2):
         turned[c] = features_ref[c].astype(F32).T.astype(BF16)
 
     def partial(c, ahead):
-        block = lax.rem(place + ahead + ring, ring)
-        at = pl.multiple_of(block * columns, columns)
-        return dot(turned[c], grad_ref[c, :, pl.ds(at, columns)])
-
-    chains = {(0, 1): half, (1, -1): half, (0, -1): half - 1, (1, 1): half - 1}
-    slot = {}
-    for key, length in chains.items():
-        for k in range(length):
-            slot[key + (k,)] = len(slot)
-    piece = rows // CHUNKS
-
-    def hop(c, way, k, j):
+        blocks[(c, ahead)].wait()
+        return dot(turned[c], grad_ref[c, :, columns_ahead(ahead)])
+
+    def pieces(c, way, k):
+        return CHUNKS
+
+    def hop(c, way, k, j=0):
         at = slot[(c, way, k)]
+        some = pl.ds(j * piece, rows // pieces(c, way, k))
         return pltpu.make_async_remote_copy(
-            src_ref=ring_send.at[j, at],
-            dst_ref=ring_recv.at[j, at],
-            send_sem=ring_out_sem.at[j, at],
-            recv_sem=ring_in_sem.at[j, at],
+            src_ref=ring_send.at[at, some],
+            dst_ref=ring_recv.at[at, some],
+            send_sem=ring_out_sem.at[at, j],
+            recv_sem=ring_in_sem.at[at, j],
             device_id=(node, right if way == 1 else left),
             device_id_type=MESH,
         )
 
     def advance(c, way, k, j):
-        at = slot[(c, way, k)]
+        at, before, some = slot[(c, way, k)], slot[(c, way, k - 1)], pl.ds(j * piece, piece)
         hop(c, way, k - 1, j).wait_recv()
-        value = parts[at, pl.ds(j * piece, piece), :] + ring_recv[j, slot[(c, way, k - 1)]].astype(F32)
-        ring_send[j, at] = value.astype(BF16)
+        ring_send[at, some] = (parts[at, some] + ring_recv[before, some].astype(F32)).astype(BF16)
         hop(c, way, k, j).start()
 
     for c, way in chains:
-        value = partial(c, way * chains[(c, way)]).astype(BF16)
-        for j in range(CHUNKS):
-            ring_send[j, slot[(c, way, 0)]] = value[j * piece : (j + 1) * piece]
+        ring_send[slot[(c, way, 0)]] = partial(c, way * chains[(c, way)]).astype(BF16)
     pl.semaphore_wait(barrier, 2 + len(close))
     for j in range(CHUNKS):
         for c, way in chains:
@@ -220,7 +240,7 @@
             device_id_type=MESH,
         )
 
-    for load in loads[2:]:
+    for load in loads[1:]:
         load.wait()
     redundant = old_owner_ref.shape[1]
     slots = experts + redundant
@@ -241,20 +261,26 @@
         state_send[:, a] = picked.reshape(nodes, 8, LANES).astype(BF16)
     state_recv[node] = state_send[node]
     state_up_to(0, 1)
-    last_step = (half - 1) * CHUNKS - 1
     heard = 0
+
+    def listen(heard):
+        if heard == farthest - 1:
+            return heard
+        heard += 1
+        hear(heard)
+        if heard < farthest - 1:
+            tell(heard + 1)
+        state_up_to(heard + 1, heard + 1)
+        return heard
+
     for k in range(1, half):
         for j in range(CHUNKS):
             for c, way in chains:
                 if k < chains[(c, way)]:
                     advance(c, way, k, j)
-            due = ((k - 1) * CHUNKS + j + 1) * (farthest - 1) // (last_step + 1)
+            due = ((k - 1) * CHUNKS + j + 1) * (farthest - 1) // ((half - 1) * CHUNKS)
             while heard < due:
-                heard += 1
-                hear(heard)
-                if heard < farthest - 1:
-                    tell(heard + 1)
-                state_up_to(heard + 1, heard + 1)
+                heard = listen(heard)
         if k == 1:
             at_old = equal(position, old_place_ref[...]).astype(BF16)
             held_new = dot_nt(at_new, expert_of_slot(new_owner_ref[...], 1)).astype(BF16)
@@ -267,10 +293,10 @@
             order[0] = equal(tall_column, (r // 2) * 8 + q * 2 + r % 2).astype(BF16)
             owner = (r % piece) // 2 * CHUNKS + r // piece
             order[1] = equal(tall_column, owner * 8 + q * 2 + r % 2).astype(BF16)
-            short = 4 * piece
-            short_row, short_column = iota((short, short), 0), iota((short, short), 1)
-            q, r = short_column // piece, short_column % piece
-            piece_order[...] = equal(short_row, (r // 2) * 8 + q * 2 + r % 2).astype(BF16)
+            low = 4 * piece
+            low_row, low_column = iota((low, low), 0), iota((low, low), 1)
+            q, r = low_column // piece, low_column % piece
+            piece_order[...] = equal(low_row, (r // 2) * 8 + q * 2 + r % 2).astype(BF16)
 
     group = nodes // CHUNKS
     line = group // CHIPS_X
@@ -292,7 +318,7 @@
             for way in (1, -1):
                 k = chains[(c, way)] - 1
                 hop(c, way, k, j).wait_recv()
-                value = value + ring_recv[j, slot[(c, way, k)]].astype(F32)
+                value = value + ring_recv[slot[(c, way, k)], pl.ds(j * piece, piece), :].astype(F32)
             value = value.astype(BF16)
             for h in range(2):
                 total[j, pl.ds((2 * c + h) * piece, piece), :] = value[:, h * LANES : (h + 1) * LANES]
@@ -315,32 +341,40 @@
 
     rows_recv[node] = rows_send[lax.rem(node, CHUNKS), node // CHUNKS]
 
-    def natural(block, out, which):
-        value = dot(order[which], block.astype(F32).reshape(tall, LANES).astype(BF16))
+    outs = (out_weight, out_first, out_second, out_grad)
+    stores = [pltpu.make_async_copy(ready.at[a], outs[a], store_sem.at[a]) for a in range(4)]
+
+    def natural(block, a):
+        value = dot(order[a // 3], block.astype(F32).reshape(tall, LANES).astype(BF16))
         for c in range(2):
             for h in range(2):
-                out[c, :, h * LANES : (h + 1) * LANES] = value[
+                outs[a][c, :, h * LANES : (h + 1) * LANES] = value[
                     (2 * c + h) * rows : (2 * c + h + 1) * rows
                 ].astype(BF16)
 
     all_but_one(state_send, state_recv, 0).wait_recv()
-    for a, out in enumerate((out_weight, out_first, out_second)):
-        natural(state_recv[:, a], out, 0)
+    for a in range(3):
+        natural(state_recv[:, a], a)
 
     all_but_one(rows_recv, rows_recv, 1).wait_recv()
-    summed = dot(match[...], rows_recv[...].astype(F32).reshape(tall, LANES).astype(BF16))
-    slots_send[...] = summed.reshape(nodes, 8, LANES).astype(BF16)
-    scatter(slots_send, slots_recv, 2, offsets)
+    owned = rows_recv[...].astype(F32).reshape(tall, LANES).astype(BF16)
+    stretch = nodes // CHIPS_X
+    for dx in sorted(range(CHIPS_X), key=lambda dx: -min(dx, CHIPS_X - dx)):
+        to_x = lax.rem(x + dx, CHIPS_X)
+        at = pl.multiple_of(to_x * (8 * stretch), 8 * stretch)
+        summed = dot(match[pl.ds(at, 8 * stretch), :], owned)
+        slots_send[pl.ds(to_x * stretch, stretch)] = summed.reshape(stretch, 8, LANES).astype(BF16)
+        scatter(slots_send, slots_recv, 2, [o for o in offsets if o[0] == dx])
     slots_recv[node] = slots_send[node]
 
     for key, length in chains.items():
         for k in range(length):
-            for j in range(CHUNKS):
+            for j in range(pieces(*key, k)):
                 hop(*key, k, j).wait_send()
     all_but_one(state_send, state_recv, 0).wait_send()
     all_but_one(rows_recv, rows_recv, 1).wait_send()
     all_but_one(slots_send, slots_recv, 2).wait_recv()
-    natural(slots_recv[...], out_grad, 1)
+    natural(slots_recv[...], 3)
     all_but_one(slots_send, slots_recv, 2).wait_send()
 
 
@@ -378,19 +412,23 @@
         features.reshape(2, features.shape[2], rows),
         grad_out.reshape(2, grad_out.shape[2], grad_out.shape[3]),
     )
-    vmem = pl.BlockSpec(memory_space=pltpu.VMEM)
-    block = jax.ShapeDtypeStruct((2, rows, columns), BF16)
+    hbm = pl.BlockSpec(memory_space=pltpu.HBM)
+    operands = tuple(pltpu.with_memory_space_constraint(x, pltpu.HBM) for x in operands)
+    block = pltpu.VMEM((2, rows, columns), BF16)
     weight_old, first_old, second_old, gradient = pl.pallas_call(
         functools.partial(exchange, nodes, ring),
         out_shape=(block,) * 4,
-        in_specs=[pl.BlockSpec(memory_space=pltpu.HBM)] * len(operands),
-        out_specs=(vmem,) * 4,
+        in_specs=[hbm] * len(operands),
+        out_specs=(pl.BlockSpec(memory_space=pltpu.VMEM),) * 4,
         scratch_shapes=[
             *(pltpu.VMEM(operand.shape, operand.dtype) for operand in operands),
             pltpu.SemaphoreType.DMA((len(operands),)),
+            pltpu.SemaphoreType.DMA((hops + 2,)),
+            pltpu.SemaphoreType.DMA((4,)),
+            pltpu.VMEM((4, 2, rows, columns), BF16),
             pltpu.VMEM((2, rows, features.shape[2]), BF16),
-            pltpu.VMEM((CHUNKS, hops, piece, columns), BF16),
-            pltpu.VMEM((CHUNKS, hops, piece, columns), BF16),
+            pltpu.VMEM((hops, rows, columns), BF16),
+            pltpu.VMEM((hops, rows, columns), BF16),
             pltpu.VMEM((nodes, 3, 8, LANES), BF16),
             pltpu.VMEM((nodes, 3, 8, LANES), BF16),
             pltpu.VMEM((CHUNKS, nodes // CHUNKS, 8, LANES), BF16),
@@ -402,14 +440,14 @@
             pltpu.VMEM((4 * piece, 4 * piece), BF16),
             pltpu.VMEM((2, tall, tall), BF16),
             pltpu.VMEM((tall, tall), BF16),
-            pltpu.SemaphoreType.DMA((CHUNKS, hops)),
-            pltpu.SemaphoreType.DMA((CHUNKS, hops)),
+            pltpu.SemaphoreType.DMA((hops, CHUNKS)),
+            pltpu.SemaphoreType.DMA((hops, CHUNKS)),
             pltpu.SemaphoreType.DMA((3,)),
             pltpu.SemaphoreType.DMA((3,)),
             pltpu.SemaphoreType.REGULAR((CHIPS_X // 2 + CHIPS_Z // 2 - 1,)),
         ],
         compiler_params=pltpu.CompilerParams(
-            collective_id=0, has_side_effects=True, vmem_limit_bytes=60 * 1024 * 1024
+            collective_id=0, has_side_effects=True, vmem_limit_bytes=40 * 1024 * 1024
         ),
         name="exchange",
     )(*operands)

time: 45.9 us -> 43.8 us (0.954)
  other arithmetic: 2.08 us -> 0.99 us
  Pallas kernels: 43 us -> 42 us
    convert_element_type x1, other arithmetic: 2.08 us -> 0.99 us  [local(): weight_new = (weight_old - LEARNING_RATE * update).astype(BF16)]
    pallas_call x1, Pallas kernels: 43 us -> 42 us  [local(): pl.pallas_call(functools.partial(exchange, nodes, ring), out_shape=(block...]
where the time goes in v4:
time: 43.8 us; the launch traced here: 43.6 us
  Pallas kernels  42 us (96%)
  other arithmetic  0.99 us (2%)
  between operations  0.64 us (1%)
    pallas_call x1, Pallas kernels, local(): pl.pallas_call(functools.partial(exchange, nodes, ring), out_shape=(block...  42 us
    convert_element_type x1, other arithmetic, local(): weight_new = (weight_old - LEARNING_RATE * update).astype(BF16)  0.99 us

profile of v4, /device:TPU:1, one launch (start us, length us, event | category | flops | bytes accessed | tf_op | source)
XLA Modules:
  0.0 43.6 jit_solution(14696324954416948812)
XLA Ops:
  0.6 42.0 %exchange.1 = (bf16[2,128,256]{2,1,0:T(8,128)(2,1)S(1)}, bf16[2,128,256]{2,1,0:T(8,128)(2,1)S(1)}, bf16[2,128,256]{2,1,0:T(8,128)(2,1)S(1)}, bf16[2,128,256]{2,1,0:T(8,128)(2,1)S(1)}) custom-call(s32[1,80]{1,0:T(1,128)} %bitcast.26, s32[1,80]{1,0:T(1,128)} %bitcast.27, s32[1,16]{1,0:T(1,128)} %bitcast.28, s32[1,16]{1,0:T(1,128)} %bitcast.29, ...), custom_call_target="tpu_custom_call" | custom-call | tf_op jit(solution)/shard_map/exchange/pallas_call | solution.py:418
  42.7 1.0 %fusion.2 = (bf16[2,128,256]{2,1,0:T(8,128)(2,1)}, f32[2,128,256]{2,1,0:T(8,128)}, f32[2,128,256]{2,1,0:T(8,128)}) fusion(bf16[2,128,256]{2,1,0:T(8,128)(2,1)S(1)} %get-tuple-element.7, bf16[2,128,256]{2,1,0:T(8,128)(2,1)S(1)} %get-tuple-element.9, bf16[2,128,256]{2,1,0:T(8,128)(2,1)S(1)} %get-tuple-element.8, bf16[2,128,256]{2,1,0:T(8,128)(2,1)S(1)} %get-tuple-element.10), kind=kLoop, calls=%fused_computation.6 | loop fusion | flops 1310720 | bytes 1179648 | tf_op jit(solution)/shard_map/convert_element_type | solution.py:462

commit v5 on v4

--- a/solution.py
+++ b/solution.py
@@ -66,8 +66,6 @@
     grad_ref,
     load_sem,
     block_sem,
-    store_sem,
-    ready,
     turned,
     ring_send,
     ring_recv,
@@ -130,7 +128,9 @@
     barrier = pltpu.get_barrier_semaphore()
     right = lax.rem(place + 1, ring)
     left = lax.rem(place + ring - 1, ring)
-    for neighbour in (right, left):
+    right_two = lax.rem(place + 2, ring)
+    left_two = lax.rem(place + ring - 2, ring)
+    for neighbour in (right, left, right_two, left_two):
         pl.semaphore_signal(barrier, inc=1, device_id=(node, neighbour), device_id_type=MESH)
     close = [(0, 0, 1)] + [(dx, dz, dc) for dx, dz in next_to for dc in range(2)]
     for offset in close:
@@ -181,18 +181,19 @@
         blocks[(c, ahead)].wait()
         return dot(turned[c], grad_ref[c, :, columns_ahead(ahead)])
 
-    def pieces(c, way, k):
-        return CHUNKS
-
     def hop(c, way, k, j=0):
         at = slot[(c, way, k)]
-        some = pl.ds(j * piece, rows // pieces(c, way, k))
+        if (c, way) in long and k == half - 2:
+            to = right_two if way == 1 else left_two
+        else:
+            to = right if way == 1 else left
+        some = pl.ds(j * piece, piece)
         return pltpu.make_async_remote_copy(
             src_ref=ring_send.at[at, some],
             dst_ref=ring_recv.at[at, some],
             send_sem=ring_out_sem.at[at, j],
             recv_sem=ring_in_sem.at[at, j],
-            device_id=(node, right if way == 1 else left),
+            device_id=(node, to),
             device_id_type=MESH,
         )
 
@@ -204,13 +205,15 @@
 
     for c, way in chains:
         ring_send[slot[(c, way, 0)]] = partial(c, way * chains[(c, way)]).astype(BF16)
-    pl.semaphore_wait(barrier, 2 + len(close))
+    pl.semaphore_wait(barrier, 4 + len(close))
     for j in range(CHUNKS):
         for c, way in chains:
             hop(c, way, 0, j).start()
     tell(1)
     for (c, way, k), at in slot.items():
-        if k:
+        if k == half - 1:
+            ring_send[at] = partial(c, way).astype(BF16)
+        elif k:
             parts[at] = partial(c, way * (chains[(c, way)] - k))
     for c in range(2):
         parts[slot[(c, 1, 0)]] = partial(c, 0)
@@ -273,12 +276,14 @@
         state_up_to(heard + 1, heard + 1)
         return heard
 
-    for k in range(1, half):
+    for k in range(1, half - 1):
         for j in range(CHUNKS):
             for c, way in chains:
-                if k < chains[(c, way)]:
-                    advance(c, way, k, j)
-            due = ((k - 1) * CHUNKS + j + 1) * (farthest - 1) // ((half - 1) * CHUNKS)
+                advance(c, way, k, j)
+            if k == half - 2:
+                for c, way in long:
+                    hop(c, way, half - 1, j).start()
+            due = ((k - 1) * CHUNKS + j + 1) * (farthest - 1) // ((half - 2) * CHUNKS)
             while heard < due:
                 heard = listen(heard)
         if k == 1:
@@ -315,10 +320,10 @@
     for j in range(CHUNKS):
         for c in range(2):
             value = parts[slot[(c, 1, 0)], pl.ds(j * piece, piece), :]
-            for way in (1, -1):
-                k = chains[(c, way)] - 1
-                hop(c, way, k, j).wait_recv()
-                value = value + ring_recv[slot[(c, way, k)], pl.ds(j * piece, piece), :].astype(F32)
+            for key in [(c, 1, half - 2), (c, -1, half - 2), (c, 1, half - 1), (c, -1, half - 1)]:
+                if key in slot:
+                    hop(*key, j).wait_recv()
+                    value = value + ring_recv[slot[key], pl.ds(j * piece, piece), :].astype(F32)
             value = value.astype(BF16)
             for h in range(2):
                 total[j, pl.ds((2 * c + h) * piece, piece), :] = value[:, h * LANES : (h + 1) * LANES]
@@ -342,7 +347,6 @@
     rows_recv[node] = rows_send[lax.rem(node, CHUNKS), node // CHUNKS]
 
     outs = (out_weight, out_first, out_second, out_grad)
-    stores = [pltpu.make_async_copy(ready.at[a], outs[a], store_sem.at[a]) for a in range(4)]
 
     def natural(block, a):
         value = dot(order[a // 3], block.astype(F32).reshape(tall, LANES).astype(BF16))
@@ -369,7 +373,7 @@
 
     for key, length in chains.items():
         for k in range(length):
-            for j in range(pieces(*key, k)):
+            for j in range(CHUNKS):
                 hop(*key, k, j).wait_send()
     all_but_one(state_send, state_recv, 0).wait_send()
     all_but_one(rows_recv, rows_recv, 1).wait_send()
@@ -424,8 +428,6 @@
             *(pltpu.VMEM(operand.shape, operand.dtype) for operand in operands),
             pltpu.SemaphoreType.DMA((len(operands),)),
             pltpu.SemaphoreType.DMA((hops + 2,)),
-            pltpu.SemaphoreType.DMA((4,)),
-            pltpu.VMEM((4, 2, rows, columns), BF16),
             pltpu.VMEM((2, rows, features.shape[2]), BF16),
             pltpu.VMEM((hops, rows, columns), BF16),
             pltpu.VMEM((hops, rows, columns), BF16),

time: 43.8 us -> 42.7 us (0.975)
  Pallas kernels: 42 us -> 40.9 us
    pallas_call x1, Pallas kernels: 42 us -> 40.9 us  [local(): pl.pallas_call(functools.partial(exchange, nodes, ring), out_shape=(block...]
where the time goes in v5:
time: 42.7 us; the launch traced here: 42.5 us
  Pallas kernels  40.9 us (96%)
  other arithmetic  0.99 us (2%)
  between operations  0.64 us (1%)
    pallas_call x1, Pallas kernels, local(): pl.pallas_call(functools.partial(exchange, nodes, ring), out_shape=(block...  40.9 us
    convert_element_type x1, other arithmetic, local(): weight_new = (weight_old - LEARNING_RATE * update).astype(BF16)  0.99 us

profile of v5, /device:TPU:1, one launch (start us, length us, event | category | flops | bytes accessed | tf_op | source)
XLA Modules:
  0.0 42.5 jit_solution(879747844949927139)
XLA Ops:
  0.6 40.9 %exchange.1 = (bf16[2,128,256]{2,1,0:T(8,128)(2,1)S(1)}, bf16[2,128,256]{2,1,0:T(8,128)(2,1)S(1)}, bf16[2,128,256]{2,1,0:T(8,128)(2,1)S(1)}, bf16[2,128,256]{2,1,0:T(8,128)(2,1)S(1)}) custom-call(s32[1,80]{1,0:T(1,128)} %bitcast.26, s32[1,80]{1,0:T(1,128)} %bitcast.27, s32[1,16]{1,0:T(1,128)} %bitcast.28, s32[1,16]{1,0:T(1,128)} %bitcast.29, ...), custom_call_target="tpu_custom_call" | custom-call | tf_op jit(solution)/shard_map/exchange/pallas_call | solution.py:422
  41.5 1.0 %fusion.2 = (bf16[2,128,256]{2,1,0:T(8,128)(2,1)}, f32[2,128,256]{2,1,0:T(8,128)}, f32[2,128,256]{2,1,0:T(8,128)}) fusion(bf16[2,128,256]{2,1,0:T(8,128)(2,1)S(1)} %get-tuple-element.7, bf16[2,128,256]{2,1,0:T(8,128)(2,1)S(1)} %get-tuple-element.9, bf16[2,128,256]{2,1,0:T(8,128)(2,1)S(1)} %get-tuple-element.8, bf16[2,128,256]{2,1,0:T(8,128)(2,1)S(1)} %get-tuple-element.10), kind=kLoop, calls=%fused_computation.6 | loop fusion | flops 1310720 | bytes 1179648 | tf_op jit(solution)/shard_map/convert_element_type | solution.py:464

commit v6 on v5

--- a/solution.py
+++ b/solution.py
@@ -17,7 +17,7 @@
 
 MESH = pl.DeviceIdType.MESH
 LANES = 128
-CHUNKS = 4
+CHUNKS = 2
 CHIPS_X, CHIPS_Z = 4, 8
 F32 = jnp.float32
 BF16 = jnp.bfloat16
@@ -276,6 +276,7 @@
         state_up_to(heard + 1, heard + 1)
         return heard
 
+    heard = listen(heard)
     for k in range(1, half - 1):
         for j in range(CHUNKS):
             for c, way in chains:

time: 42.7 us -> 42.2 us (0.988)
  Pallas kernels: 40.9 us -> 40.4 us
    pallas_call x1, Pallas kernels: 40.9 us -> 40.4 us  [local(): pl.pallas_call(functools.partial(exchange, nodes, ring), out_shape=(block...]
where the time goes in v6:
time: 42.2 us; the launch traced here: 42 us
  Pallas kernels  40.4 us (96%)
  other arithmetic  0.99 us (2%)
  between operations  0.64 us (2%)
    pallas_call x1, Pallas kernels, local(): pl.pallas_call(functools.partial(exchange, nodes, ring), out_shape=(block...  40.4 us
    convert_element_type x1, other arithmetic, local(): weight_new = (weight_old - LEARNING_RATE * update).astype(BF16)  0.99 us

profile of v6, /device:TPU:1, one launch (start us, length us, event | category | flops | bytes accessed | tf_op | source)
XLA Modules:
  0.0 42.0 jit_solution(17251559701119718816)
XLA Ops:
  0.6 40.4 %exchange.1 = (bf16[2,128,256]{2,1,0:T(8,128)(2,1)S(1)}, bf16[2,128,256]{2,1,0:T(8,128)(2,1)S(1)}, bf16[2,128,256]{2,1,0:T(8,128)(2,1)S(1)}, bf16[2,128,256]{2,1,0:T(8,128)(2,1)S(1)}) custom-call(s32[1,80]{1,0:T(1,128)} %bitcast.26, s32[1,80]{1,0:T(1,128)} %bitcast.27, s32[1,16]{1,0:T(1,128)} %bitcast.28, s32[1,16]{1,0:T(1,128)} %bitcast.29, ...), custom_call_target="tpu_custom_call" | custom-call | tf_op jit(solution)/shard_map/exchange/pallas_call | solution.py:423
  41.0 1.0 %fusion.2 = (bf16[2,128,256]{2,1,0:T(8,128)(2,1)}, f32[2,128,256]{2,1,0:T(8,128)}, f32[2,128,256]{2,1,0:T(8,128)}) fusion(bf16[2,128,256]{2,1,0:T(8,128)(2,1)S(1)} %get-tuple-element.7, bf16[2,128,256]{2,1,0:T(8,128)(2,1)S(1)} %get-tuple-element.9, bf16[2,128,256]{2,1,0:T(8,128)(2,1)S(1)} %get-tuple-element.8, bf16[2,128,256]{2,1,0:T(8,128)(2,1)S(1)} %get-tuple-element.10), kind=kLoop, calls=%fused_computation.6 | loop fusion | flops 1310720 | bytes 1179648 | tf_op jit(solution)/shard_map/convert_element_type | solution.py:465

commit v7 on v6

--- a/solution.py
+++ b/solution.py
@@ -284,7 +284,7 @@
             if k == half - 2:
                 for c, way in long:
                     hop(c, way, half - 1, j).start()
-            due = ((k - 1) * CHUNKS + j + 1) * (farthest - 1) // ((half - 2) * CHUNKS)
+            due = min(farthest - 1, 1 + ((k - 1) * CHUNKS + j + 1) * (farthest - 1) // ((half - 2) * CHUNKS))
             while heard < due:
                 heard = listen(heard)
         if k == 1:

time: 42.2 us -> 42.6 us (level)
  no operation moved by 1% of the time
where the time goes in v7:
time: 42.6 us; the launch traced here: 42.4 us
  Pallas kernels  40.8 us (96%)
  other arithmetic  0.99 us (2%)
  between operations  0.64 us (2%)
    pallas_call x1, Pallas kernels, local(): pl.pallas_call(functools.partial(exchange, nodes, ring), out_shape=(block...  40.8 us
    convert_element_type x1, other arithmetic, local(): weight_new = (weight_old - LEARNING_RATE * update).astype(BF16)  0.99 us

profile of v7, /device:TPU:1, one launch (start us, length us, event | category | flops | bytes accessed | tf_op | source)
XLA Modules:
  0.0 42.4 jit_solution(3784807721802726237)
XLA Ops:
  0.6 40.8 %exchange.1 = (bf16[2,128,256]{2,1,0:T(8,128)(2,1)S(1)}, bf16[2,128,256]{2,1,0:T(8,128)(2,1)S(1)}, bf16[2,128,256]{2,1,0:T(8,128)(2,1)S(1)}, bf16[2,128,256]{2,1,0:T(8,128)(2,1)S(1)}) custom-call(s32[1,80]{1,0:T(1,128)} %bitcast.26, s32[1,80]{1,0:T(1,128)} %bitcast.27, s32[1,16]{1,0:T(1,128)} %bitcast.28, s32[1,16]{1,0:T(1,128)} %bitcast.29, ...), custom_call_target="tpu_custom_call" | custom-call | tf_op jit(solution)/shard_map/exchange/pallas_call | solution.py:423
  41.4 1.0 %fusion.2 = (bf16[2,128,256]{2,1,0:T(8,128)(2,1)}, f32[2,128,256]{2,1,0:T(8,128)}, f32[2,128,256]{2,1,0:T(8,128)}) fusion(bf16[2,128,256]{2,1,0:T(8,128)(2,1)S(1)} %get-tuple-element.7, bf16[2,128,256]{2,1,0:T(8,128)(2,1)S(1)} %get-tuple-element.9, bf16[2,128,256]{2,1,0:T(8,128)(2,1)S(1)} %get-tuple-element.8, bf16[2,128,256]{2,1,0:T(8,128)(2,1)S(1)} %get-tuple-element.10), kind=kLoop, calls=%fused_computation.6 | loop fusion | flops 1310720 | bytes 1179648 | tf_op jit(solution)/shard_map/convert_element_type | solution.py:465
